TPU v7x, 256 devices: a whole 4x4x8 slice. The times are simulated.
256 devices in a mesh: ch: 4 (over x_hi, core), tile: 64 (over y, z, x_lo).
Axes of the slice: x: 4 (x_hi: 2, x_lo: 2; x = x_hi * 2 + x_lo), y: 4, z: 8, core: 2. Of those that a mesh axis runs over, the one named last changes fastest.
Arguments:
- frames: bfloat16 [2, 64, 32, 56, 512], P(None, 'tile', None, None, 'ch'), may hold values from -6 to 6
- cached: bfloat16 [2, 64, 32, 56, 512], P(None, 'tile', None, None, 'ch'), may hold values from -6 to 6
- weight: bfloat16 [3, 3, 3, 512, 512], P(None, None, None, 'ch'), may hold values from -0.0546875 to 0.0546875
- out_bias: float32 [512], P('ch'), may hold values from -3 to 3
Outputs:
- activated: bfloat16 [2, 64, 32, 56, 512], P(None, 'tile', None, None, 'ch')
All inputs are finite; a program needn't handle non-finite values.
Results may differ from a plain program's by a relative error of at most 0.0023.
Values may be sent and summed in bfloat16 or wider, within the bound.
A program may use at most 64 MiB of HBM per device.

v0:
```python
import jax
import jax.numpy as jnp
from jax import lax
from jax.sharding import PartitionSpec as P

GX = 8


def passed_along(x, axis, by):
    size = lax.axis_size(axis)
    pairs = [(i, i + by) for i in range(size) if 0 <= i + by < size]
    return lax.ppermute(x, axis, pairs)


def shards(frames, cached, weight, out_bias):
    stacked = jnp.concatenate([cached[:, 0], frames[:, 0]], axis=0)
    column = lax.axis_index("tile") % GX

    def usable(shifted, offset):
        if offset == 1:
            keep = column > 0
        else:
            keep = column < GX - 1
        return jnp.where(keep, shifted, jnp.zeros_like(shifted))

    def side_input(field, offset):
        return usable(passed_along(field, "tile", offset), offset)

    def end_input(field, offset):
        return passed_along(field, "tile", offset)

    from_left = side_input(stacked[:, :, -1:, :], 1)
    from_right = side_input(stacked[:, :, :1, :], -1)
    widened = jnp.concatenate([from_left, stacked, from_right], axis=2)
    from_above = end_input(widened[:, -1:], GX)
    from_below = end_input(widened[:, :1], -GX)
    padded = jnp.concatenate([from_above, widened, from_below], axis=1)
    window = padded[None]
    product = lax.conv_general_dilated(
        window,
        weight,
        (1, 1, 1),
        "VALID",
        dimension_numbers=("NDHWC", "DHWIO", "NDHWC"),
        preferred_element_type=jnp.float32,
    )
    summed = lax.psum_scatter(product[0], "ch", scatter_dimension=3, tiled=True)
    activated = jax.nn.silu(summed + out_bias[None, None, None, :]).astype(jnp.bfloat16)
    return activated[:, None]


def solution(mesh):
    in_specs = (
        P(None, "tile", None, None, "ch"),
        P(None, "tile", None, None, "ch"),
        P(None, None, None, "ch", None),
        P("ch"),
    )
    out_specs = P(None, "tile", None, None, "ch")
    return jax.shard_map(shards, mesh=mesh, in_specs=in_specs, out_specs=out_specs, check_vma=False)
```

profile of v0, /device:TPU:1, one launch (start us, length us, event | category | flops | bytes accessed | tf_op | source)
XLA Modules:
  0.0 160.8 jit_solution(9731453540774993039)
XLA Ops:
  6.5 0.0 copy-start
  6.5 0.0 reduce-scatter.2.cloned.1.call-start
  6.5 2.0 %pad_maximum_fusion.5 = (bf16[4,32,1,128]{3,2,1,0:T(2,128)(2,1)}, bf16[4,32,1,128]{3,2,1,0:T(2,128)(2,1)}) fusion(bf16[2,32,56,128]{3,2,1,0:T(8,128)(2,1)} %bitcast.20, bf16[2,32,56,128]{3,2,1,0:T(8,128)(2,1)} %bitcast.23), kind=kLoop, calls=%fused_computation.22 | loop fusion | flops 131072 | bytes 1900544 | tf_op jit(solution)/shard_map/slice | solution.py:32
  8.6 4.6 %collective-permute-start = (bf16[4,32,1,128]{3,2,1,0:T(2,128)(2,1)}, bf16[4,32,1,128]{3,2,1,0:T(2,128)(2,1)}, u32[]{:S(2)}, u32[]{:S(2)}) collective-permute-start(bf16[4,32,1,128]{3,2,1,0:T(2,128)(2,1)} %get-tuple-element.7), channel_id=1, source_target_pairs={{0,1},{1,2},{2,3},{3,4},{4,5},{5,6},{6,7},{7,8},{8,9},{9,10},{10,1... | collective-permute-start | bytes 98312 | tf_op jit(solution)/shard_map/ppermute | solution.py:12
  13.1 1.3 collective-permute-start.1
  14.4 0.0 copy-start.1
  14.4 0.0 copy-start.2
  14.4 0.0 collective-permute-done
  14.5 0.1 broadcast_select_fusion.2
  14.5 3.9 %collective-permute-done.1 = bf16[4,32,1,128]{3,2,1,0:T(2,128)(2,1)} collective-permute-done((bf16[4,32,1,128]{3,2,1,0:T(2,128)(2,1)}, bf16[4,32,1,128]{3,2,1,0:T(2,128)(2,1)}, u32[]{:S(2)}, u32[]{:S(2)}) %collective-permute-start.1) | collective-permute-done | bytes 32800 | tf_op jit(solution)/shard_map/ppermute | solution.py:12
  18.4 0.9 broadcast_select_fusion.1
  19.4 0.9 pad_maximum_fusion.3
  20.2 8.9 %collective-permute-start.2 = (bf16[4,1,58,128]{3,2,1,0:T(8,128)(2,1)S(1)}, bf16[4,1,58,128]{3,2,1,0:T(8,128)(2,1)S(1)}, u32[]{:S(2)}, u32[]{:S(2)}) collective-permute-start(bf16[4,1,58,128]{3,2,1,0:T(8,128)(2,1)S(1)} %get-tuple-element.5), channel_id=1, source_target_pairs={{0,8},{1,9},{2,10},{3,11},{4,12},{5,13},{6,14},{7,15},{8,16},{9,17... | collective-permute-start | bytes 178184 | tf_op jit(solution)/shard_map/ppermute | solution.py:12
  29.1 1.3 collective-permute-start.3
  30.4 0.1 collective-permute-done.2
  30.6 7.5 %collective-permute-done.3 = bf16[4,1,58,128]{3,2,1,0:T(8,128)(2,1)S(1)} collective-permute-done((bf16[4,1,58,128]{3,2,1,0:T(8,128)(2,1)S(1)}, bf16[4,1,58,128]{3,2,1,0:T(8,128)(2,1)S(1)}, u32[]{:S(2)}, u32[]{:S(2)}) %collective-permute-start.3) | collective-permute-done | bytes 59424 | tf_op jit(solution)/shard_map/ppermute | solution.py:12
  38.0 0.0 copy-done.1
  38.0 0.0 copy-done.2
  38.1 1.8 %maximum_bitcast_fusion = bf16[4,34,1,58,128]{4,3,1,0,2:T(8,128)(2,1)S(1)} fusion(bf16[4,1,58,128]{3,2,1,0:T(8,128)(2,1)S(1)} %collective-permute-done.3, bf16[4,32,1,128]{3,2,1,0:T(2,128)(2,1)S(1)} %broadcast_select_fusion.1, bf16[2,32,56,128]{3,2,1,0:T(8,128)(2,1)S(1)} %bitcast.22, bf16[2,32,56,128]{3,2,1,0:T(8,128)(2,1)S(1)} %bitcast.25, ...), kind=kLoop, calls=%fused_computation.10 | loop fusion | flops 12115968 | bytes 4038656 | tf_op jit(solution)/shard_map/broadcast_in_dim | solution.py:38
  39.9 0.5 pad_bitcast_fusion
  40.4 0.0 copy-start.4
  40.4 0.7 copy.6
  41.1 0.1 slice.18
  41.3 0.0 copy-done
  41.3 0.0 copy-done.4
  41.3 17.3 %broadcast_select_fusion = f32[2,32,8,8,512]{4,2,3,1,0:T(8,128)S(1)} fusion(pred[8,8]{0,1:T(8,128)(4,1)S(1)} %copy-done.4, bf16[3,3,3,128,512]{4,3,2,1,0:T(8,128)(2,1)S(1)} %copy-done, bf16[4,34,1,7,2,128]{5,3,4,1,0,2:T(8,128)(2,1)S(1)} %slice.18, bf16[4,34,1,8,8,128]{5,3,4,1,0,2:T(8,128)(2,1)S(1)} %copy.6), kind=kOutput, calls=%fused_computation.4 | convolution fusion | flops 14505967616 | bytes 14643264 | tf_op jit(solution)/shard_map/conv_general_dilated | solution.py:39
  58.6 8.1 %copy.10 = f32[2,32,8,8,512]{4,3,2,1,0:T(8,128)S(1)} copy(f32[2,32,8,8,512]{4,2,3,1,0:T(8,128)S(1)} %broadcast_select_fusion) | data formatting | bytes 16777216 | tf_op jit(solution)/shard_map/conv_general_dilated | solution.py:39
  66.7 3.8 %slice_bitcast_fusion = f32[2,32,56,512]{3,2,1,0:T(8,128)} fusion(f32[2,32,1,64,512]{4,3,1,0,2:T(8,128)S(1)} %bitcast.19), kind=kLoop, calls=%fused_computation.1 | loop fusion | bytes 14680064 | tf_op jit(solution)/shard_map/squeeze | solution.py:47
  70.5 0.0 reduce-scatter.2.cloned.1.call-update
  70.6 80.4 %reduce-scatter.2.cloned.1.call-done = f32[2,32,56,128]{3,2,1,0:T(8,128)} async-done(((f32[2,32,56,512]{3,2,1,0:T(8,128)}), f32[2,32,56,128]{3,2,1,0:T(8,128)}) %reduce-scatter.2.cloned.1.call-update) | async-done | bytes 1835024 | tf_op jit(solution)/shard_map/reduce_scatter | solution.py:47
  151.0 0.0 copy-done.3
  151.0 2.9 %fusion.8 = bf16[2,1,32,56,128]{4,3,2,1,0:T(8,128)(2,1)} fusion(f32[2,32,56,128]{3,2,1,0:T(8,128)} %reduce-scatter.2.cloned.1.call-done, f32[128]{0:T(128)S(1)} %copy-done.3), kind=kLoop, calls=%fused_computation.14 | loop fusion | flops 2752512 | bytes 2753024 | tf_op jit(solution)/shard_map/broadcast_in_dim | solution.py:49
  (1 shorter events, 0.0 us)
Async XLA Ops:
  6.5 34.7 %copy-start = (bf16[3,3,3,128,512]{4,3,2,1,0:T(8,128)(2,1)S(1)}, bf16[3,3,3,128,512]{4,3,2,1,0:T(8,128)(2,1)}, u32[]{:S(2)}) copy-start(bf16[3,3,3,128,512]{4,3,2,1,0:T(8,128)(2,1)} %param.6) | copy-start | bytes 10616836
  6.5 144.5 %reduce-scatter.2.cloned.1.call-start = ((), (), s32[]{:S(2)}) async-start(), calls=%async_computation.1 | async-start | bytes 9175040 | tf_op jit(solution)/shard_map/reduce_scatter | solution.py:47
  8.6 5.9 %collective-permute-start = (bf16[4,32,1,128]{3,2,1,0:T(2,128)(2,1)}, bf16[4,32,1,128]{3,2,1,0:T(2,128)(2,1)}, u32[]{:S(2)}, u32[]{:S(2)}) collective-permute-start(bf16[4,32,1,128]{3,2,1,0:T(2,128)(2,1)} %get-tuple-element.7), channel_id=1, source_target_pairs={{0,1},{1,2},{2,3},{3,4},{4,5},{5,6},{6,7},{7,8},{8,9},{9,10},{10,1... | collective-permute-start | bytes 98312 | tf_op jit(solution)/shard_map/ppermute | solution.py:12
  13.1 5.3 %collective-permute-start.1 = (bf16[4,32,1,128]{3,2,1,0:T(2,128)(2,1)}, bf16[4,32,1,128]{3,2,1,0:T(2,128)(2,1)}, u32[]{:S(2)}, u32[]{:S(2)}) collective-permute-start(bf16[4,32,1,128]{3,2,1,0:T(2,128)(2,1)} %get-tuple-element.8), channel_id=1, source_target_pairs={{1,0},{2,1},{3,2},{4,3},{5,4},{6,5},{7,6},{8,7},{9,8},{10,9},{11,1... | collective-permute-start | bytes 98312 | tf_op jit(solution)/shard_map/ppermute | solution.py:12
  14.4 23.6 %copy-start.1 = (bf16[2,1,32,56,128]{4,3,2,1,0:T(8,128)(2,1)S(1)}, bf16[2,1,32,56,128]{4,3,2,1,0:T(8,128)(2,1)}, u32[]{:S(2)}) copy-start(bf16[2,1,32,56,128]{4,3,2,1,0:T(8,128)(2,1)} %param.4) | copy-start | bytes 2752516
  14.4 23.6 %copy-start.2 = (bf16[2,1,32,56,128]{4,3,2,1,0:T(8,128)(2,1)S(1)}, bf16[2,1,32,56,128]{4,3,2,1,0:T(8,128)(2,1)}, u32[]{:S(2)}) copy-start(bf16[2,1,32,56,128]{4,3,2,1,0:T(8,128)(2,1)} %param.5) | copy-start | bytes 2752516
  20.2 10.4 %collective-permute-start.2 = (bf16[4,1,58,128]{3,2,1,0:T(8,128)(2,1)S(1)}, bf16[4,1,58,128]{3,2,1,0:T(8,128)(2,1)S(1)}, u32[]{:S(2)}, u32[]{:S(2)}) collective-permute-start(bf16[4,1,58,128]{3,2,1,0:T(8,128)(2,1)S(1)} %get-tuple-element.5), channel_id=1, source_target_pairs={{0,8},{1,9},{2,10},{3,11},{4,12},{5,13},{6,14},{7,15},{8,16},{9,17... | collective-permute-start | bytes 178184 | tf_op jit(solution)/shard_map/ppermute | solution.py:12
  29.1 8.9 %collective-permute-start.3 = (bf16[4,1,58,128]{3,2,1,0:T(8,128)(2,1)S(1)}, bf16[4,1,58,128]{3,2,1,0:T(8,128)(2,1)S(1)}, u32[]{:S(2)}, u32[]{:S(2)}) collective-permute-start(bf16[4,1,58,128]{3,2,1,0:T(8,128)(2,1)S(1)} %get-tuple-element.6), channel_id=1, source_target_pairs={{8,0},{9,1},{10,2},{11,3},{12,4},{13,5},{14,6},{15,7},{16,8},{17,9... | collective-permute-start | bytes 178184 | tf_op jit(solution)/shard_map/ppermute | solution.py:12
  40.4 0.9 copy-start.4
  70.5 80.5 %copy-start.3 = (f32[128]{0:T(128)S(1)}, f32[128]{0:T(128)}, u32[]{:S(2)}) copy-start(f32[128]{0:T(128)} %param.7) | copy-start | bytes 1540
Sparse Core Ops, SparseCore 0:
  70.7 80.2 reduce-scatter.1
where the time goes:
time: 161 us
  waiting for transfers between devices  92 us (57%)
  matrix products  17.3 us (11%)
  starting transfers between devices  16.1 us (10%)
  between operations  13.5 us (8%)
  local copies, waits for them, and re-layouts  13.3 us (8%)
  other arithmetic  8.62 us (5%)
    reduce_scatter x1, waiting for transfers between devices, shards(): summed = lax.psum_scatter(product[0], 'ch', scatter_dimension=3, tiled=True)  80.4 us
    conv_general_dilated x1, matrix products, shards(): lax.conv_general_dilated(window, weight, (1, 1, 1), 'VALID', dimension_nu...  17.3 us
    ppermute x4, starting transfers between devices, passed_along(): return lax.ppermute(x, axis, pairs)  16 us
    ppermute x4, waiting for transfers between devices, passed_along(): return lax.ppermute(x, axis, pairs)  11.5 us
    conv_general_dilated x4, local copies, waits for them, and re-layouts, shards(): lax.conv_general_dilated(window, weight, (1, 1, 1), 'VALID', dimension_nu...  9.44 us
    squeeze x1, local copies, waits for them, and re-layouts, shards(): summed = lax.psum_scatter(product[0], 'ch', scatter_dimension=3, tiled=True)  3.84 us
  transfers between devices with their start and end apart: 5, of which 4 were waited for; matrix products, arithmetic and copies ran while one was open for 0% of the time, Pallas kernels for 0%

commit v1 on v0

v1 whole, which is shorter than its diff:
```python
import jax
import jax.numpy as jnp
from jax import lax
from jax.experimental import pallas as pl
from jax.experimental.pallas import tpu as pltpu
from jax.sharding import PartitionSpec as P

GX = 8
GY = 8
TH = 32
TW = 56
CB = 128
PIX = TH * TW
RB = 4
NB = TH // RB
BR = RB * TW
MB = 2 * BR
PAIR = 2 * TW
SCALE = 2.0**20
MESH = pl.DeviceIdType.MESH
TAPS = [(a, b, e) for a in range(3) for b in range(3) for e in range(3)]


def encode(v):
    s = v * SCALE
    return ((s * s) * (s * jnp.abs(s))).astype(jnp.bfloat16)


def decode(w):
    w = w.astype(jnp.float32)
    root = jnp.sqrt(jnp.sqrt(jnp.abs(w))) * (1.0 / SCALE)
    return jnp.where(w < 0, -root, root)


def sideways(v, left, right):
    lane = lax.broadcasted_iota(jnp.int32, (8, CB), 0)
    m = pltpu.roll(v, 1, 0)
    p = pltpu.roll(v, TW - 1, 0)
    m = jnp.concatenate([jnp.where(lane == 0, left, m[:8]), m[8:]], axis=0)
    p = jnp.concatenate([p[:-8], jnp.where(lane == 7, right, p[-8:])], axis=0)
    return m, v, p


def kernel(cached, frames, weight, bias, out, xe, xo, wr, wl, edge_l, edge_r, halo_l, halo_r, left_f, right_f, halo_a, halo_b,
           corner_up, corner_dn, corner_a, corner_b, core_out, core_in, keep, cross_out, cross_in, out_v,
           in_sem, halo_ss, halo_rs, core_ss, core_rs, cross_ss, cross_rs, out_sem):
    ch = lax.axis_index("ch")
    tile = lax.axis_index("tile")
    h, c = ch // 2, ch % 2
    row, col = tile // GX, tile % GX
    left = (ch, row * GX + (col + GX - 1) % GX)
    right = (ch, row * GX + (col + 1) % GX)
    up = (ch, ((row + GY - 1) % GY) * GX + col)
    down = (ch, ((row + 1) % GY) * GX + col)
    mate = (h * 2 + (1 - c), tile)
    across = ((1 - h) * 2 + c, tile)

    loads = [
        pltpu.make_async_copy(cached, xo.at[1, pl.ds(0, 2)], in_sem.at[0]),
        pltpu.make_async_copy(frames, xo.at[1, pl.ds(2, 2)], in_sem.at[1]),
    ]
    for i, (dst, half, group) in enumerate([(wr, 0, (1 - h) * 2 + 1 - c), (wr, 1, (1 - h) * 2 + c), (wl, 0, h * 2 + 1 - c), (wl, 1, ch)]):
        loads.append(pltpu.make_async_copy(
            weight.at[:, pl.ds(pl.multiple_of(group * CB, CB), CB)], dst.at[:, pl.ds(half * CB, CB)], in_sem.at[2 + i]))
    for load in loads:
        load.start()

    barrier = pltpu.get_barrier_semaphore()
    for device in (left, right, up, down, mate, across):
        pl.semaphore_signal(barrier, inc=1, device_id=device, device_id_type=MESH)
    loads[0].wait()
    loads[1].wait()

    lane = lax.broadcasted_iota(jnp.int32, (8, CB), 0)

    @pl.loop(0, 4)
    def _(f):
        for g in range(2):
            acc_l = [jnp.zeros((8, CB), jnp.float32)] * 2
            acc_r = [jnp.zeros((8, CB), jnp.float32)] * 2
            for q in range(8):
                at = (g * 8 + q) * PAIR
                first = xo[1, f, at:at + 16, :].astype(jnp.float32)
                middle = xo[1, f, at + 48:at + 64, :].astype(jnp.float32)
                last = xo[1, f, at + 96:at + 112, :].astype(jnp.float32)
                k, d = (2 * q) // 8, (2 * q) % 8
                acc_l[k] = jnp.where(lane == d, first[0:1], acc_l[k])
                acc_r[k] = jnp.where(lane == d, middle[7:8], acc_r[k])
                acc_l[k] = jnp.where(lane == d + 1, middle[8:9], acc_l[k])
                acc_r[k] = jnp.where(lane == d + 1, last[15:16], acc_r[k])
            at = pl.ds(pl.multiple_of(f * TH + g * 16, 16), 16)
            edge_l[at, :] = jnp.concatenate(acc_l, axis=0).astype(jnp.bfloat16)
            edge_r[at, :] = jnp.concatenate(acc_r, axis=0).astype(jnp.bfloat16)

    pl.semaphore_wait(barrier, 6)

    def remote(src, dst, ss, rs, device):
        return pltpu.make_async_remote_copy(src_ref=src, dst_ref=dst, send_sem=ss, recv_sem=rs, device_id=device, device_id_type=MESH)

    to_left = remote(edge_l, halo_r, halo_ss.at[0], halo_rs.at[0], left)
    to_right = remote(edge_r, halo_l, halo_ss.at[1], halo_rs.at[1], right)
    to_up = remote(xo.at[1, :, pl.ds(0, 64)], halo_b, halo_ss.at[2], halo_rs.at[2], up)
    to_down = remote(xo.at[1, :, pl.ds(PIX - 64, 64)], halo_a, halo_ss.at[3], halo_rs.at[3], down)
    to_left.start()
    to_right.start()
    to_up.start()
    to_down.start()
    to_left.wait_recv()
    to_right.wait_recv()
    left_f[...] = jnp.where(col > 0, halo_l[...].astype(jnp.float32), 0.0)
    right_f[...] = jnp.where(col < GX - 1, halo_r[...].astype(jnp.float32), 0.0)

    for ref, r in ((corner_up, 0), (corner_dn, TH - 1)):
        pieces = []
        for f in range(4):
            pieces += [left_f[f * TH + r:f * TH + r + 1, :], right_f[f * TH + r:f * TH + r + 1, :]]
        ref[...] = jnp.concatenate(pieces + [jnp.zeros((8, CB), jnp.float32)], axis=0).astype(jnp.bfloat16)
    corner_to_up = remote(corner_up, corner_b, halo_ss.at[4], halo_rs.at[4], up)
    corner_to_down = remote(corner_dn, corner_a, halo_ss.at[5], halo_rs.at[5], down)
    corner_to_up.start()
    corner_to_down.start()

    def real_row(v, f, r):
        return sideways(v, left_f[pl.ds(f * TH + r, 1), :], right_f[pl.ds(f * TH + r, 1), :])

    def put(ref, f, q, one, two, which):
        at = pl.ds(pl.multiple_of(q * PAIR, 16), PAIR)
        for e in which:
            ref[e, f, at, :] = jnp.concatenate([one[e], two[e]], axis=0).astype(jnp.bfloat16)

    def own_pair(f, q):
        v = xo[1, f, pl.ds(pl.multiple_of(q * PAIR, 16), PAIR), :].astype(jnp.float32)
        return real_row(v[:TW], f, 2 * q), real_row(v[TW:], f, 2 * q + 1)

    def second_of(f, q):
        v = xo[1, f, pl.ds(pl.multiple_of(q * PAIR + 48, 16), 64), :].astype(jnp.float32)
        return real_row(v[8:], f, 2 * q + 1)

    def build(f, q):
        above = second_of(f, q - 1)
        one, two = own_pair(f, q)
        put(xe, f, q, above, one, (0, 1, 2))
        put(xo, f, q, one, two, (0, 2))

    def block(w, core_slot, core, b):
        base = b * BR
        parts = []
        for a, y, e in TAPS:
            ref = xo if y == 1 else xe
            at = pl.multiple_of(base + (PAIR if y == 2 else 0), 16)
            parts.append(ref[e, a:a + 2, pl.ds(at, BR), :].reshape(MB, CB))
        product = jnp.dot(jnp.concatenate(parts, axis=1), w[...], preferred_element_type=jnp.float32)
        core_out[core_slot, b] = product[:, :CB]
        core(b).start()
        keep[b] = product[:, CB:]

    def core_far(b):
        return remote(core_out.at[0, b], core_in.at[0, b], core_ss.at[0, b], core_rs.at[0, b], mate)

    def core_near(b):
        return remote(core_out.at[1, b], core_in.at[1, b], core_ss.at[1, b], core_rs.at[1, b], mate)

    def cross(b):
        return remote(cross_out.at[b], cross_in.at[b], cross_ss.at[b], cross_rs.at[b], across)

    def pass_on(b):
        core_far(b).wait_recv()
        cross_out[b] = encode(keep[b] + core_in[0, b])
        cross(b).start()

    @pl.loop(0, 8)
    def _(i):
        build(i % 4, 2 + i // 4)

    loads[2].wait()
    loads[3].wait()

    @pl.loop(1, NB - 1)
    def _(b):
        @pl.loop(0, 4)
        def _(f):
            build(f, 2 * b + 2)

            @pl.when(b > 1)
            def _():
                build(f, 2 * b + 1)

        block(wr, 0, core_far, b)

        @pl.when(b > 1)
        def _():
            pass_on(b - 1)

    to_up.wait_recv()
    to_down.wait_recv()
    corner_to_up.wait_recv()
    corner_to_down.wait_recv()

    def corner(ref, f, keep_it):
        pair = jnp.where(keep_it, ref[...].astype(jnp.float32), 0.0)
        return pair[2 * f:2 * f + 1], pair[2 * f + 1:2 * f + 2]

    for f in range(4):
        v = jnp.where(row > 0, halo_a[f].astype(jnp.float32)[8:], 0.0)
        above = sideways(v, *corner(corner_a, f, row > 0))
        one, two = own_pair(f, 0)
        put(xe, f, 0, above, one, (0, 1, 2))
        put(xo, f, 0, one, two, (0, 2))
        build(f, 1)
    block(wr, 0, core_far, 0)
    pass_on(NB - 2)
    for f in range(4):
        build(f, TH // 2 - 1)
        v = jnp.where(row < GY - 1, halo_b[f].astype(jnp.float32)[:TW], 0.0)
        below = sideways(v, *corner(corner_b, f, row < GY - 1))
        put(xe, f, TH // 2, second_of(f, TH // 2 - 1), below, (0, 1, 2))
    block(wr, 0, core_far, NB - 1)
    pass_on(0)
    loads[4].wait()
    loads[5].wait()
    pass_on(NB - 1)

    @pl.loop(0, NB)
    def _(b):
        block(wl, 1, core_near, b)

    def store(b):
        at = pl.ds(pl.multiple_of(b * BR, 16), BR)
        return pltpu.make_async_copy(out_v.at[:, at], out.at[:, at], out_sem.at[b])

    @pl.loop(1, NB + 1)
    def _(i):
        b = jnp.where(i == NB, NB - 1, jnp.where(i == NB - 1, 0, i))
        core_near(b).wait_recv()
        cross(b).wait_recv()
        v = keep[b] + core_in[1, b] + decode(cross_in[b]) + bias[...]
        v = v / (1.0 + jnp.exp(-v))
        out_v[:, pl.ds(pl.multiple_of(b * BR, 16), BR), :] = v.astype(jnp.bfloat16).reshape(2, BR, CB)
        store(b).start()

    for copy in (to_left, to_right, to_up, to_down, corner_to_up, corner_to_down):
        copy.wait_send()

    @pl.loop(0, NB)
    def _(b):
        core_far(b).wait_send()
        core_near(b).wait_send()
        cross(b).wait_send()
        store(b).wait()


def shards(frames, cached, weight, out_bias):
    anywhere = pl.BlockSpec(memory_space=pl.ANY)
    bf16, f32 = jnp.bfloat16, jnp.float32
    out = pl.pallas_call(
        kernel,
        out_shape=jax.ShapeDtypeStruct((2, PIX, CB), bf16),
        in_specs=[anywhere, anywhere, anywhere, pl.BlockSpec(memory_space=pltpu.VMEM)],
        out_specs=anywhere,
        scratch_shapes=[
            pltpu.VMEM((3, 4, PIX + PAIR, CB), bf16),
            pltpu.VMEM((3, 4, PIX, CB), bf16),
            pltpu.VMEM((27 * CB, 2 * CB), bf16),
            pltpu.VMEM((27 * CB, 2 * CB), bf16),
            *[pltpu.VMEM((4 * TH, CB), bf16)] * 4,
            *[pltpu.VMEM((4 * TH, CB), f32)] * 2,
            *[pltpu.VMEM((4, 64, CB), bf16)] * 2,
            *[pltpu.VMEM((16, CB), bf16)] * 4,
            pltpu.VMEM((2, NB, MB, CB), f32),
            pltpu.VMEM((2, NB, MB, CB), f32),
            pltpu.VMEM((NB, MB, CB), f32),
            pltpu.VMEM((NB, MB, CB), bf16),
            pltpu.VMEM((NB, MB, CB), bf16),
            pltpu.VMEM((2, PIX, CB), bf16),
            pltpu.SemaphoreType.DMA((6,)),
            pltpu.SemaphoreType.DMA((6,)),
            pltpu.SemaphoreType.DMA((6,)),
            pltpu.SemaphoreType.DMA((2, NB)),
            pltpu.SemaphoreType.DMA((2, NB)),
            pltpu.SemaphoreType.DMA((NB,)),
            pltpu.SemaphoreType.DMA((NB,)),
            pltpu.SemaphoreType.DMA((NB,)),
        ],
        compiler_params=pltpu.CompilerParams(collective_id=0, has_side_effects=True, vmem_limit_bytes=48 << 20),
        cost_estimate=pl.CostEstimate(flops=2 * 2 * PIX * 27 * CB * 4 * CB, bytes_accessed=7 << 20, transcendentals=2 * PIX * CB),
        name="conv",
    )(
        cached.reshape(2, PIX, CB),
        frames.reshape(2, PIX, CB),
        weight.reshape(27 * CB, 4 * CB),
        out_bias.reshape(1, CB),
    )
    return out.reshape(2, 1, TH, TW, CB)


def solution(mesh):
    in_specs = (
        P(None, "tile", None, None, "ch"),
        P(None, "tile", None, None, "ch"),
        P(None, None, None, "ch", None),
        P("ch"),
    )
    out_specs = P(None, "tile", None, None, "ch")
    return jax.shard_map(shards, mesh=mesh, in_specs=in_specs, out_specs=out_specs, check_vma=False)
```

time: 161 us -> 47.4 us (0.29)
  waiting for transfers between devices: 92 us -> 0 us
  Pallas kernels: 0 us -> 43.3 us
  matrix products: 17.3 us -> 0 us
  starting transfers between devices: 16.1 us -> 0 us
  between operations: 13.5 us -> 0.01 us
  local copies, waits for them, and re-layouts: 13.3 us -> 3.94 us
  other arithmetic: 8.62 us -> 0 us
    reduce_scatter x1 -> x0, waiting for transfers between devices: 80.4 us -> none  [shards(): summed = lax.psum_scatter(product[0], 'ch', scatter_dimension=3, tiled=True)]
    pallas_call x0 -> x1, Pallas kernels: none -> 43.3 us  [shards(): pl.pallas_call(kernel, out_shape=jax.ShapeDtypeStruct((2, PIX, CB), bf16)...]
    conv_general_dilated x1 -> x0, matrix products: 17.3 us -> none  [shards(): lax.conv_general_dilated(window, weight, (1, 1, 1), 'VALID', dimension_nu...]
    ppermute x4 -> x0, starting transfers between devices: 16 us -> none  [passed_along(): return lax.ppermute(x, axis, pairs)]
    ppermute x4 -> x0, waiting for transfers between devices: 11.5 us -> none  [passed_along(): return lax.ppermute(x, axis, pairs)]
    conv_general_dilated x4 -> x0, local copies, waits for them, and re-layouts: 9.44 us -> none  [shards(): lax.conv_general_dilated(window, weight, (1, 1, 1), 'VALID', dimension_nu...]
    broadcast_in_dim x2 -> x0, other arithmetic: 4.76 us -> none  [the longest x1 2.91 us: shards(): return activated[:, None]]
    unnamed x10 -> x7, local copies, waits for them, and re-layouts: 0.03 us -> 3.94 us
  transfers between devices with their start and end apart: 5 -> 0, of which waited for: 4 -> 0; matrix products, arithmetic and copies ran while one was open for 0% -> 0% of each run, Pallas kernels for 0% -> 0%
where the time goes in v1:
time: 47.4 us; the launch traced here: 47.3 us
  Pallas kernels  43.3 us (91%)
  local copies, waits for them, and re-layouts  3.94 us (8%)
    pallas_call x1, Pallas kernels, shards(): pl.pallas_call(kernel, out_shape=jax.ShapeDtypeStruct((2, PIX, CB), bf16)...  43.3 us
    unnamed x7, local copies, waits for them, and re-layouts  3.94 us

profile of v1, /device:TPU:1, one launch (start us, length us, event | category | flops | bytes accessed | tf_op | source)
XLA Modules:
  0.0 47.3 jit_solution(7311147779331758844)
XLA Ops:
  0.0 0.0 copy-start
  0.0 1.2 %copy-done = bf16[2,1,32,56,128]{4,3,2,1,0:T(8,128)(2,1)S(1)} copy-done((bf16[2,1,32,56,128]{4,3,2,1,0:T(8,128)(2,1)S(1)}, bf16[2,1,32,56,128]{4,3,2,1,0:T(8,128)(2,1)}, u32[]{:S(2)}) %copy-start) | copy-done | bytes 917528
  1.2 0.0 copy-start.1
  1.2 1.2 %copy-done.1 = bf16[2,1,32,56,128]{4,3,2,1,0:T(8,128)(2,1)S(1)} copy-done((bf16[2,1,32,56,128]{4,3,2,1,0:T(8,128)(2,1)S(1)}, bf16[2,1,32,56,128]{4,3,2,1,0:T(8,128)(2,1)}, u32[]{:S(2)}) %copy-start.1) | copy-done | bytes 917528
  2.4 0.0 copy-start.2
  2.4 0.7 %copy-done.2 = f32[128]{0:T(128)S(1)} copy-done((f32[128]{0:T(128)S(1)}, f32[128]{0:T(128)}, u32[]{:S(2)}) %copy-start.2) | copy-done | bytes 536
  3.0 43.3 %conv.1 = bf16[2,1792,128]{2,1,0:T(8,128)(2,1)S(1)} custom-call(bf16[2,1792,128]{2,1,0:T(8,128)(2,1)S(1)} %bitcast.8, bf16[2,1792,128]{2,1,0:T(8,128)(2,1)S(1)} %bitcast.9, bf16[3456,512]{1,0:T(8,128)(2,1)} %bitcast.11, f32[1,128]{1,0:T(1,128)S(1)} %bitcast.10), custom_call_target="tpu_custom_call" | custom-call | flops 12683575296 | bytes 7340032 | tf_op jit(solution)/shard_map/conv/pallas_call | solution.py:255
  46.3 0.9 %copy.7 = bf16[2,1,32,56,128]{4,3,2,1,0:T(8,128)(2,1)} copy(bf16[2,1,32,56,128]{4,3,2,1,0:T(8,128)(2,1)S(1)} %bitcast.7) | data formatting | bytes 1835008
Async XLA Ops:
  0.0 1.2 %copy-start = (bf16[2,1,32,56,128]{4,3,2,1,0:T(8,128)(2,1)S(1)}, bf16[2,1,32,56,128]{4,3,2,1,0:T(8,128)(2,1)}, u32[]{:S(2)}) copy-start(bf16[2,1,32,56,128]{4,3,2,1,0:T(8,128)(2,1)} %param.5) | copy-start | bytes 2752516
  1.2 1.2 %copy-start.1 = (bf16[2,1,32,56,128]{4,3,2,1,0:T(8,128)(2,1)S(1)}, bf16[2,1,32,56,128]{4,3,2,1,0:T(8,128)(2,1)}, u32[]{:S(2)}) copy-start(bf16[2,1,32,56,128]{4,3,2,1,0:T(8,128)(2,1)} %param.4) | copy-start | bytes 2752516
  2.4 0.7 %copy-start.2 = (f32[128]{0:T(128)S(1)}, f32[128]{0:T(128)}, u32[]{:S(2)}) copy-start(f32[128]{0:T(128)} %param.7) | copy-start | bytes 1540

commit v2 on v0

v2 whole, which is shorter than its diff:
```python
import jax
import jax.numpy as jnp
from jax import lax
from jax.experimental import pallas as pl
from jax.experimental.pallas import tpu as pltpu
from jax.sharding import PartitionSpec as P

GX = 8
GY = 8
TH = 32
TW = 56
CB = 128
PIX = TH * TW
PAIR = 2 * TW
NP = TH // 2
SCALE = 2.0**20
MESH = pl.DeviceIdType.MESH
TAPS = [(a, b, e) for a in range(3) for b in range(3) for e in range(3)]
INNER = [(16, 32), (64, 32)]
RIM = [(0, 16), (48, 16), (96, 16)]
WHOLE = [(0, PAIR)]
INNER_ROWS, RIM_ROWS, END_ROWS = 2 * 64, 2 * 48, 2 * PAIR
MIDDLE = NP - 2
RIM_AT = MIDDLE * INNER_ROWS
END_AT = RIM_AT + MIDDLE * RIM_ROWS
ROWS = END_AT + 2 * END_ROWS
FIRST = [(0, 2), (2, 2), (4, 5), (9, 5)]
HALF = MIDDLE // 2


def encode(v):
    s = v * SCALE
    return ((s * s) * (s * jnp.abs(s))).astype(jnp.bfloat16)


def decode(w):
    w = w.astype(jnp.float32)
    root = jnp.sqrt(jnp.sqrt(jnp.abs(w))) * (1.0 / SCALE)
    return jnp.where(w < 0, -root, root)


def sideways(v):
    return pltpu.roll(v, 1, 0), v, pltpu.roll(v, TW - 1, 0)


def ends(moved, left, right):
    m, v, p = moved
    lane = lax.broadcasted_iota(jnp.int32, (8, CB), 0)
    m = jnp.concatenate([jnp.where(lane == 0, left, m[:8]), m[8:]], axis=0)
    p = jnp.concatenate([p[:-8], jnp.where(lane == 7, right, p[-8:])], axis=0)
    return m, v, p


def aligned(i):
    return i if isinstance(i, int) else pl.multiple_of(i, 16)


def kernel(cached, frames, weight, bias_in, out, xe, xo, w, bias, edge_l, edge_r, halo_l, halo_r, left_f, right_f, halo_a, halo_b,
           corner_up, corner_dn, corner_a, corner_b, core_out, core_in, keep, cross_out, cross_in,
           in_sem, halo_ss, halo_rs, far_ss, far_rs, near_ss, near_rs, cross_ss, cross_rs):
    ch = lax.axis_index("ch")
    tile = lax.axis_index("tile")
    h, c = ch // 2, ch % 2
    row, col = tile // GX, tile % GX
    left = (ch, row * GX + (col + GX - 1) % GX)
    right = (ch, row * GX + (col + 1) % GX)
    up = (ch, ((row + GY - 1) % GY) * GX + col)
    down = (ch, ((row + 1) % GY) * GX + col)
    mate = (h * 2 + (1 - c), tile)
    across = ((1 - h) * 2 + c, tile)

    loads = [
        pltpu.make_async_copy(cached, xo.at[1, pl.ds(0, 2)], in_sem.at[0]),
        pltpu.make_async_copy(frames, xo.at[1, pl.ds(2, 2)], in_sem.at[1]),
    ]
    for i, group in enumerate([(1 - h) * 2 + 1 - c, (1 - h) * 2 + c, h * 2 + 1 - c, ch]):
        loads.append(pltpu.make_async_copy(
            weight.at[:, pl.ds(pl.multiple_of(group * CB, CB), CB)], w.at[:, pl.ds(i * CB, CB)], in_sem.at[2 + i]))
    loads.append(pltpu.make_async_copy(bias_in, bias, in_sem.at[6]))
    for load in loads:
        load.start()

    barrier = pltpu.get_barrier_semaphore()
    for device in (left, right, up, down, mate, across):
        pl.semaphore_signal(barrier, inc=1, device_id=device, device_id_type=MESH)
    loads[0].wait()
    loads[1].wait()

    def put(ref, f, q, one, two, which):
        at = pl.ds(aligned(q * PAIR), PAIR)
        for e in which:
            ref[e, f, at, :] = jnp.concatenate([one[e], two[e]], axis=0).astype(jnp.bfloat16)

    def own_pair(f, q):
        v = xo[1, f, pl.ds(aligned(q * PAIR), PAIR), :].astype(jnp.float32)
        return sideways(v[:TW]), sideways(v[TW:])

    def second_of(f, q):
        return sideways(xo[1, f, pl.ds(aligned(q * PAIR + 48), 64), :].astype(jnp.float32)[8:])

    def build(f, q):
        above = second_of(f, q - 1)
        one, two = own_pair(f, q)
        put(xe, f, q, above, one, (0, 1, 2))
        put(xo, f, q, one, two, (0, 2))

    def build_all(q0, q1):
        @pl.loop(0, 4 * (q1 - q0))
        def _(i):
            build(i % 4, q0 + i // 4)

    def remote(src, dst, ss, rs, device):
        return pltpu.make_async_remote_copy(src_ref=src, dst_ref=dst, send_sem=ss, recv_sem=rs, device_id=device, device_id_type=MESH)

    def far_core(i, at, n):
        at = pl.ds(aligned(at), n)
        return remote(core_out.at[0, at], core_in.at[0, at], far_ss.at[i], far_rs.at[i], mate)

    def near_core(i, at, n):
        at = pl.ds(aligned(at), n)
        return remote(core_out.at[1, at], core_in.at[1, at], near_ss.at[i], near_rs.at[i], mate)

    def cross(i, at, n):
        at = pl.ds(aligned(at), n)
        return remote(cross_out.at[at], cross_in.at[at], cross_ss.at[i], cross_rs.at[i], across)

    def pass_on(i, at, n):
        far_core(i, at, n).wait_recv()
        rows = pl.ds(aligned(at), n)
        cross_out[rows, :] = encode(keep[0, rows, :] + core_in[0, rows, :])
        cross(i, at, n).start()

    def product(qs, segments, sides, at):
        columns = []
        for a, y, e in TAPS:
            ref = xo if y == 1 else xe
            pieces = []
            for q in qs:
                for start, n in segments:
                    rows = pl.ds(aligned(q * PAIR + start + (PAIR if y == 2 else 0)), n)
                    pieces.append(ref[e, a:a + 2, rows, :].reshape(2 * n, CB))
            columns.append(jnp.concatenate(pieces, axis=0) if len(pieces) > 1 else pieces[0])
        first = sides[0] * 2 * CB
        sums = jnp.dot(
            jnp.concatenate(columns, axis=1), w[:, first:first + len(sides) * 2 * CB], preferred_element_type=jnp.float32)
        rows = pl.ds(aligned(at), sums.shape[0])
        for k, side in enumerate(sides):
            core_out[side, rows, :] = sums[:, 2 * k * CB:(2 * k + 1) * CB]
            keep[side, rows, :] = sums[:, (2 * k + 1) * CB:(2 * k + 2) * CB]

    def inner(i0, n, sides):
        product([1 + i0 + k for k in range(n)], INNER, sides, i0 * INNER_ROWS)

    inner_rows = [(i, i0 * INNER_ROWS, n * INNER_ROWS) for i, (i0, n) in enumerate(FIRST)]
    end_rows = (6, END_AT, 2 * END_ROWS)

    def rim_rows(i):
        return 4 + i, RIM_AT + i * HALF * RIM_ROWS, HALF * RIM_ROWS

    lane = lax.broadcasted_iota(jnp.int32, (8, CB), 0)

    @pl.loop(0, 4)
    def _(f):
        for g in range(2):
            acc_l = [jnp.zeros((8, CB), jnp.float32)] * 2
            acc_r = [jnp.zeros((8, CB), jnp.float32)] * 2
            for q in range(8):
                at = (g * 8 + q) * PAIR
                start = xo[1, f, at:at + 16, :].astype(jnp.float32)
                middle = xo[1, f, at + 48:at + 64, :].astype(jnp.float32)
                last = xo[1, f, at + 96:at + 112, :].astype(jnp.float32)
                k, d = (2 * q) // 8, (2 * q) % 8
                acc_l[k] = jnp.where(lane == d, start[0:1], acc_l[k])
                acc_r[k] = jnp.where(lane == d, middle[7:8], acc_r[k])
                acc_l[k] = jnp.where(lane == d + 1, middle[8:9], acc_l[k])
                acc_r[k] = jnp.where(lane == d + 1, last[15:16], acc_r[k])
            at = pl.ds(pl.multiple_of(f * TH + g * 16, 16), 16)
            edge_l[at, :] = jnp.concatenate(acc_l, axis=0).astype(jnp.bfloat16)
            edge_r[at, :] = jnp.concatenate(acc_r, axis=0).astype(jnp.bfloat16)

    build_all(1, 4)
    loads[2].wait()
    loads[3].wait()
    inner(*FIRST[0], [0])
    pl.semaphore_wait(barrier, 6)
    far_core(*inner_rows[0]).start()

    to_left = remote(edge_l, halo_r, halo_ss.at[0], halo_rs.at[0], left)
    to_right = remote(edge_r, halo_l, halo_ss.at[1], halo_rs.at[1], right)
    to_up = remote(xo.at[1, :, pl.ds(0, 64)], halo_b, halo_ss.at[2], halo_rs.at[2], up)
    to_down = remote(xo.at[1, :, pl.ds(PIX - 64, 64)], halo_a, halo_ss.at[3], halo_rs.at[3], down)
    to_left.start()
    to_right.start()
    to_up.start()
    to_down.start()

    build_all(4, 6)
    inner(*FIRST[1], [0])
    far_core(*inner_rows[1]).start()
    build_all(6, 11)
    pass_on(*inner_rows[0])
    inner(*FIRST[2], [0])
    far_core(*inner_rows[2]).start()
    pass_on(*inner_rows[1])
    build_all(11, NP)
    inner(*FIRST[3], [0])
    far_core(*inner_rows[3]).start()
    pass_on(*inner_rows[2])

    to_left.wait_recv()
    to_right.wait_recv()
    left_f[...] = jnp.where(col > 0, halo_l[...].astype(jnp.float32), 0.0)
    right_f[...] = jnp.where(col < GX - 1, halo_r[...].astype(jnp.float32), 0.0)

    for ref, r in ((corner_up, 0), (corner_dn, TH - 1)):
        pieces = []
        for f in range(4):
            pieces += [left_f[f * TH + r:f * TH + r + 1, :], right_f[f * TH + r:f * TH + r + 1, :]]
        ref[...] = jnp.concatenate(pieces + [jnp.zeros((8, CB), jnp.float32)], axis=0).astype(jnp.bfloat16)
    corner_to_up = remote(corner_up, corner_b, halo_ss.at[4], halo_rs.at[4], up)
    corner_to_down = remote(corner_dn, corner_a, halo_ss.at[5], halo_rs.at[5], down)
    corner_to_up.start()
    corner_to_down.start()

    place = lax.broadcasted_iota(jnp.int32, (16, CB), 0)

    def side_pixels(f, r):
        at = pl.ds(f * TH + r, 1)
        return left_f[at, :], right_f[at, :]

    @pl.loop(0, 4 * (NP - 1))
    def _(i):
        f, q = i % 4, 1 + i // 4
        for ref, r in ((xe, 2 * q - 1), (xo, 2 * q)):
            one, two = side_pixels(f, r), side_pixels(f, r + 1)
            for e, start, k, pixel in ((0, 0, 0, one[0]), (0, 48, 8, two[0]), (2, 48, 7, one[1]), (2, 96, 15, two[1])):
                at = pl.ds(aligned(q * PAIR + start), 16)
                ref[e, f, at, :] = jnp.where(place == k, pixel, ref[e, f, at, :].astype(jnp.float32)).astype(jnp.bfloat16)

    pass_on(*inner_rows[3])
    loads[4].wait()
    loads[5].wait()

    @pl.loop(0, 2)
    def _(i):
        product([1 + i * HALF + k for k in range(HALF)], RIM, [0, 1], RIM_AT + i * HALF * RIM_ROWS)
        far_core(*rim_rows(i)).start()
        near_core(2 + i, *rim_rows(i)[1:]).start()

        @pl.when(i == 1)
        def _():
            pass_on(*rim_rows(0))

    to_up.wait_recv()
    to_down.wait_recv()
    corner_to_up.wait_recv()
    corner_to_down.wait_recv()

    def corner(ref, f, inside):
        pair = jnp.where(inside, ref[...].astype(jnp.float32), 0.0)
        return pair[2 * f:2 * f + 1], pair[2 * f + 1:2 * f + 2]

    for f in range(4):
        v = jnp.where(row > 0, halo_a[f].astype(jnp.float32)[8:], 0.0)
        above = ends(sideways(v), *corner(corner_a, f, row > 0))
        one, two = own_pair(f, 0)
        one, two = ends(one, *side_pixels(f, 0)), ends(two, *side_pixels(f, 1))
        put(xe, f, 0, above, one, (0, 1, 2))
        put(xo, f, 0, one, two, (0, 2))
        v = jnp.where(row < GY - 1, halo_b[f].astype(jnp.float32)[:TW], 0.0)
        below = ends(sideways(v), *corner(corner_b, f, row < GY - 1))
        put(xe, f, NP, ends(second_of(f, NP - 1), *side_pixels(f, TH - 1)), below, (0, 1, 2))
    pass_on(*rim_rows(1))
    product([0, NP - 1], WHOLE, [0, 1], END_AT)
    far_core(*end_rows).start()
    near_core(4, *end_rows[1:]).start()

    @pl.loop(0, 2)
    def _(i):
        inner(i * HALF, HALF, [1])
        near_core(i, i * HALF * INNER_ROWS, HALF * INNER_ROWS).start()

        @pl.when(i == 0)
        def _():
            pass_on(*end_rows)

    loads[6].wait()

    def finish(q, segments, at, n):
        rows = pl.ds(aligned(at), n)
        v = keep[1, rows, :] + core_in[1, rows, :] + decode(cross_in[rows, :]) + bias[...]
        v = (v / (1.0 + jnp.exp(-v))).astype(jnp.bfloat16)
        at = 0
        for start, k in segments:
            for f in range(2):
                out[f, pl.ds(aligned(q * PAIR + start), k), :] = v[at:at + k]
                at += k

    for i in range(2):
        near_core(i, i * HALF * INNER_ROWS, HALF * INNER_ROWS).wait_recv()
    for i, (i0, n) in enumerate(FIRST):
        cross(*inner_rows[i]).wait_recv()

        @pl.loop(i0, i0 + n)
        def _(k):
            finish(1 + k, INNER, k * INNER_ROWS, INNER_ROWS)

    for i in range(2):
        near_core(2 + i, *rim_rows(i)[1:]).wait_recv()
        cross(*rim_rows(i)).wait_recv()

        @pl.loop(i * HALF, (i + 1) * HALF)
        def _(k):
            finish(1 + k, RIM, RIM_AT + k * RIM_ROWS, RIM_ROWS)

    near_core(4, *end_rows[1:]).wait_recv()
    for copy in (to_left, to_right, to_up, to_down, corner_to_up, corner_to_down):
        copy.wait_send()
    for i in range(2):
        near_core(i, i * HALF * INNER_ROWS, HALF * INNER_ROWS).wait_send()
        near_core(2 + i, *rim_rows(i)[1:]).wait_send()
    near_core(4, *end_rows[1:]).wait_send()
    for rows in (*inner_rows, rim_rows(0), rim_rows(1), end_rows):
        far_core(*rows).wait_send()
    cross(*end_rows).wait_recv()
    finish(0, WHOLE, END_AT, END_ROWS)
    finish(NP - 1, WHOLE, END_AT + END_ROWS, END_ROWS)
    for rows in (*inner_rows, rim_rows(0), rim_rows(1), end_rows):
        cross(*rows).wait_send()


def shards(frames, cached, weight, out_bias):
    anywhere = pl.BlockSpec(memory_space=pl.ANY)
    bf16, f32 = jnp.bfloat16, jnp.float32
    operands = (
        cached.reshape(2, PIX, CB),
        frames.reshape(2, PIX, CB),
        weight.reshape(27 * CB, 4 * CB),
        out_bias.reshape(1, CB),
    )
    out = pl.pallas_call(
        kernel,
        out_shape=jax.ShapeDtypeStruct((2, PIX, CB), bf16),
        in_specs=[anywhere] * 4,
        out_specs=pl.BlockSpec(memory_space=pltpu.VMEM),
        scratch_shapes=[
            pltpu.VMEM((3, 4, PIX + PAIR, CB), bf16),
            pltpu.VMEM((3, 4, PIX, CB), bf16),
            pltpu.VMEM((27 * CB, 4 * CB), bf16),
            pltpu.VMEM((1, CB), f32),
            *[pltpu.VMEM((4 * TH, CB), bf16)] * 4,
            *[pltpu.VMEM((4 * TH, CB), f32)] * 2,
            *[pltpu.VMEM((4, 64, CB), bf16)] * 2,
            *[pltpu.VMEM((16, CB), bf16)] * 4,
            *[pltpu.VMEM((2, ROWS, CB), f32)] * 3,
            *[pltpu.VMEM((ROWS, CB), bf16)] * 2,
            *[pltpu.SemaphoreType.DMA((7,))] * 1,
            *[pltpu.SemaphoreType.DMA((6,))] * 2,
            *[pltpu.SemaphoreType.DMA((7,))] * 2,
            *[pltpu.SemaphoreType.DMA((5,))] * 2,
            *[pltpu.SemaphoreType.DMA((7,))] * 2,
        ],
        compiler_params=pltpu.CompilerParams(collective_id=0, has_side_effects=True, vmem_limit_bytes=48 << 20),
        cost_estimate=pl.CostEstimate(flops=2 * 2 * PIX * 27 * CB * 4 * CB, bytes_accessed=7 << 20, transcendentals=2 * PIX * CB),
        name="conv",
    )(*[pltpu.with_memory_space_constraint(x, pltpu.HBM) for x in operands])
    return out.reshape(2, 1, TH, TW, CB)


def solution(mesh):
    in_specs = (
        P(None, "tile", None, None, "ch"),
        P(None, "tile", None, None, "ch"),
        P(None, None, None, "ch", None),
        P("ch"),
    )
    out_specs = P(None, "tile", None, None, "ch")
    return jax.shard_map(shards, mesh=mesh, in_specs=in_specs, out_specs=out_specs, check_vma=False)
```

time: 161 us -> 40.3 us (0.25)
  waiting for transfers between devices: 92 us -> 0 us
  Pallas kernels: 0 us -> 39.3 us
  matrix products: 17.3 us -> 0 us
  starting transfers between devices: 16.1 us -> 0 us
  between operations: 13.5 us -> 0.01 us
  local copies, waits for them, and re-layouts: 13.3 us -> 0.93 us
  other arithmetic: 8.62 us -> 0 us
    reduce_scatter x1 -> x0, waiting for transfers between devices: 80.4 us -> none  [shards(): summed = lax.psum_scatter(product[0], 'ch', scatter_dimension=3, tiled=True)]
    pallas_call x0 -> x1, Pallas kernels: none -> 39.3 us  [shards(): pl.pallas_call(kernel, out_shape=jax.ShapeDtypeStruct((2, PIX, CB), bf16)...]
    conv_general_dilated x1 -> x0, matrix products: 17.3 us -> none  [shards(): lax.conv_general_dilated(window, weight, (1, 1, 1), 'VALID', dimension_nu...]
    ppermute x4 -> x0, starting transfers between devices: 16 us -> none  [passed_along(): return lax.ppermute(x, axis, pairs)]
    ppermute x4 -> x0, waiting for transfers between devices: 11.5 us -> none  [passed_along(): return lax.ppermute(x, axis, pairs)]
    conv_general_dilated x4 -> x0, local copies, waits for them, and re-layouts: 9.44 us -> none  [shards(): lax.conv_general_dilated(window, weight, (1, 1, 1), 'VALID', dimension_nu...]
    broadcast_in_dim x2 -> x0, other arithmetic: 4.76 us -> none  [the longest x1 2.91 us: shards(): return activated[:, None]]
    squeeze x1 -> x0, local copies, waits for them, and re-layouts: 3.84 us -> none  [shards(): summed = lax.psum_scatter(product[0], 'ch', scatter_dimension=3, tiled=True)]
  transfers between devices with their start and end apart: 5 -> 0, of which waited for: 4 -> 0; matrix products, arithmetic and copies ran while one was open for 0% -> 0% of each run, Pallas kernels for 0% -> 0%
where the time goes in v2:
time: 40.3 us
  Pallas kernels  39.3 us (98%)
  local copies, waits for them, and re-layouts  0.93 us (2%)
    pallas_call x1, Pallas kernels, shards(): pl.pallas_call(kernel, out_shape=jax.ShapeDtypeStruct((2, PIX, CB), bf16)...  39.3 us
    unnamed x1, local copies, waits for them, and re-layouts  0.93 us

profile of v2, /device:TPU:1, one launch (start us, length us, event | category | flops | bytes accessed | tf_op | source)
XLA Modules:
  0.0 40.3 jit_solution(8099415339939142970)
XLA Ops:
  0.0 39.3 %conv.1 = bf16[2,1792,128]{2,1,0:T(8,128)(2,1)S(1)} custom-call(bf16[2,1792,128]{2,1,0:T(8,128)(2,1)} %bitcast.9, bf16[2,1792,128]{2,1,0:T(8,128)(2,1)} %bitcast.10, bf16[3456,512]{1,0:T(8,128)(2,1)} %bitcast.8, f32[1,128]{1,0:T(1,128)} %bitcast.11), custom_call_target="tpu_custom_call" | custom-call | flops 12683575296 | bytes 7340032 | tf_op jit(solution)/shard_map/conv/pallas_call | solution.py:341
  39.3 0.9 %copy.7 = bf16[2,1,32,56,128]{4,3,2,1,0:T(8,128)(2,1)} copy(bf16[2,1,32,56,128]{4,3,2,1,0:T(8,128)(2,1)S(1)} %bitcast.7) | data formatting | bytes 1835008

commit v3 on v0

v3 whole, which is shorter than its diff:
```python
import jax
import jax.numpy as jnp
from jax import lax
from jax.experimental import pallas as pl
from jax.experimental.pallas import tpu as pltpu
from jax.sharding import PartitionSpec as P

GX = 8
GY = 8
TH = 32
TW = 56
CB = 128
PIX = TH * TW
PAIR = 2 * TW
NP = TH // 2
SLOTS = TW // 8
SLOT = 16
WIDE = (SLOTS + 2) * SLOT
FRAME = 8 + (TH + 2) * TW + 8
SIDE = TH + 16
SCALE = 2.0**20
MESH = pl.DeviceIdType.MESH
TAPS = [(a, b, e) for a in range(3) for b in range(3) for e in range(3)]
INNER = [(1, 5)]
RIM = [(0, 1), (6, 1)]
WHOLE = [(0, 7)]
INNER_ROWS, RIM_ROWS, END_ROWS = 2 * 5 * SLOT, 2 * 2 * SLOT, 2 * PAIR
MIDDLE = NP - 2
RIM_AT = MIDDLE * INNER_ROWS
END_AT = RIM_AT + MIDDLE * RIM_ROWS
ROWS = END_AT + 2 * END_ROWS
BLOCKS = 7
BLOCK = MIDDLE // BLOCKS
BLOCK_ROWS = BLOCK * INNER_ROWS
HALF = MIDDLE // 2
HALF_ROWS = HALF * RIM_ROWS
PARTS = BLOCKS + 4


def encode(v):
    s = v * SCALE
    return ((s * s) * (s * jnp.abs(s))).astype(jnp.bfloat16)


def decode(w):
    w = w.astype(jnp.float32)
    root = jnp.sqrt(jnp.sqrt(jnp.abs(w))) * (1.0 / SCALE)
    return jnp.where(w < 0, -root, root)


def kernel(cached, frames, weight, bias_in, out, xin, xf, xe, xo, w, bias, edge_l, edge_r, halo_l, halo_r, left_f, right_f,
           halo_a, halo_b, corner_up, corner_dn, corner_a, corner_b, core_out, core_in, keep, cross_out, cross_in, out_f,
           in_sem, halo_ss, halo_rs, core_ss, core_rs, cross_ss, cross_rs):
    ch = lax.axis_index("ch")
    tile = lax.axis_index("tile")
    h, c = ch // 2, ch % 2
    row, col = tile // GX, tile % GX
    left = (ch, row * GX + (col + GX - 1) % GX)
    right = (ch, row * GX + (col + 1) % GX)
    up = (ch, ((row + GY - 1) % GY) * GX + col)
    down = (ch, ((row + 1) % GY) * GX + col)
    mate = (h * 2 + (1 - c), tile)
    across = ((1 - h) * 2 + c, tile)

    loads = [
        pltpu.make_async_copy(cached, xin.at[pl.ds(0, 2)], in_sem.at[0]),
        pltpu.make_async_copy(frames, xin.at[pl.ds(2, 2)], in_sem.at[1]),
    ]
    for i, group in enumerate([(1 - h) * 2 + 1 - c, (1 - h) * 2 + c, h * 2 + 1 - c, ch]):
        loads.append(pltpu.make_async_copy(
            weight.at[:, pl.ds(pl.multiple_of(group * CB, CB), CB)], w.at[i // 2, :, pl.ds(i % 2 * CB, CB)], in_sem.at[2 + i]))
    loads.append(pltpu.make_async_copy(bias_in, bias, in_sem.at[6]))
    for load in loads:
        load.start()

    barrier = pltpu.get_barrier_semaphore()
    for device in (left, right, up, down, mate, across):
        pl.semaphore_signal(barrier, inc=1, device_id=device, device_id_type=MESH)

    def remote(src, dst, ss, rs, device):
        return pltpu.make_async_remote_copy(src_ref=src, dst_ref=dst, send_sem=ss, recv_sem=rs, device_id=device, device_id_type=MESH)

    def block(i):
        return i, i * BLOCK_ROWS, BLOCK_ROWS

    def half(i):
        return BLOCKS + i, RIM_AT + i * HALF_ROWS, HALF_ROWS

    def end(i):
        return BLOCKS + 2 + i, END_AT + i * END_ROWS, END_ROWS

    def rows_of(at, n):
        return pl.ds(at if isinstance(at, int) else pl.multiple_of(at, 16), n)

    def core(side, part):
        i, at, n = part
        rows = rows_of(at, n)
        return remote(core_out.at[side, rows], core_in.at[side, rows], core_ss.at[side, i], core_rs.at[side, i], mate)

    def cross(part):
        i, at, n = part
        rows = rows_of(at, n)
        return remote(cross_out.at[rows], cross_in.at[rows], cross_ss.at[i], cross_rs.at[i], across)

    def pass_on(part):
        core(0, part).wait_recv()
        rows = rows_of(*part[1:])
        cross_out[rows, :] = encode(keep[0, rows, :] + core_in[0, rows, :])
        cross(part).start()

    def place_of(f, r):
        return f * FRAME + 8 + (r + 1) * TW

    def build(ref, f, q, r):
        for k in range(SLOTS):
            v = xf[pl.ds(place_of(f, r) + k, SLOT, stride=SLOTS), :]
            ref[f, q, (k + 1) * SLOT:(k + 2) * SLOT, :] = v.astype(jnp.bfloat16)

    spot = lax.broadcasted_iota(jnp.int32, (SLOT, CB), 0)

    def build_sides(ref, f, q, r):
        for side, k, slot in ((left_f, -1, 0), (right_f, SLOTS, SLOTS + 1)):
            v = xf[pl.ds(place_of(f, r) + k, SLOT, stride=SLOTS), :]
            at = 0 if k < 0 else 7
            for j in range(2):
                v = jnp.where(spot == at + 8 * j, side[pl.ds(f * SIDE + 8 + r + j, 1), :], v)
            ref[f, q, slot * SLOT:(slot + 1) * SLOT, :] = v.astype(jnp.bfloat16)

    def build_all(q0, q1):
        @pl.loop(q0, q1)
        def _(q):
            for f in range(4):
                build(xo, f, q, 2 * q)
                build(xe, f, q, 2 * q - 1)

    def product(groups, slots, side, at):
        columns = []
        for a, y, e in TAPS:
            pieces = []
            for q, n in groups:
                for first, count in slots:
                    ref, q_at = (xo, q) if y == 1 else (xe, q + y // 2)
                    v = ref[a:a + 2, pl.ds(q_at, n), (first + e) * SLOT:(first + e + count) * SLOT, :]
                    pieces.append(v.reshape(2 * n * count * SLOT, CB))
            columns.append(jnp.concatenate(pieces, axis=0) if len(pieces) > 1 else pieces[0])
        sums = jnp.dot(jnp.concatenate(columns, axis=1), w[side], preferred_element_type=jnp.float32)
        rows = rows_of(at, sums.shape[0])
        core_out[side, rows, :] = sums[:, :CB]
        keep[side, rows, :] = sums[:, CB:]

    loads[0].wait()
    loads[1].wait()

    @pl.loop(0, NP)
    def _(q):
        for f in range(4):
            v = xin[f, pl.ds(pl.multiple_of(q * PAIR, 16), PAIR), :]
            xf[pl.ds(pl.multiple_of(place_of(f, 2 * q), 8), PAIR), :] = v.astype(jnp.float32)

    for f in range(4):
        at = f * TH
        edge_l[at:at + TH, :] = xf[pl.ds(place_of(f, 0), TH, stride=TW), :].astype(jnp.bfloat16)
        edge_r[at:at + TH, :] = xf[pl.ds(place_of(f, 0) + TW - 1, TH, stride=TW), :].astype(jnp.bfloat16)

    build_all(1, 4)
    loads[2].wait()
    loads[3].wait()
    to_left = remote(edge_l, halo_r, halo_ss.at[0], halo_rs.at[0], left)
    to_right = remote(edge_r, halo_l, halo_ss.at[1], halo_rs.at[1], right)
    to_up = remote(xin.at[:, pl.ds(0, 64)], halo_b, halo_ss.at[2], halo_rs.at[2], up)
    to_down = remote(xin.at[:, pl.ds(PIX - 64, 64)], halo_a, halo_ss.at[3], halo_rs.at[3], down)
    halos = (to_left, to_right, to_up, to_down)

    @pl.loop(0, 2 * BLOCKS)
    def _(j):
        side, b = j // BLOCKS, j % BLOCKS

        @pl.when(j == BLOCKS)
        def _():
            loads[4].wait()
            loads[5].wait()

        product([(1 + b * BLOCK, BLOCK)], INNER, side, b * BLOCK_ROWS)

        @pl.when(j == 0)
        def _():
            pl.semaphore_wait(barrier, 6)
            core(side, block(b)).start()
            for halo in halos:
                halo.start()

        @pl.when(j > 0)
        def _():
            core(side, block(b)).start()

        @pl.when(j < BLOCKS - 1)
        def _():
            build_all(2 + (b + 1) * BLOCK, 2 + (b + 2) * BLOCK)

        @pl.when((j > 0) & (j <= BLOCKS))
        def _():
            pass_on(block(j - 1))

    to_left.wait_recv()
    to_right.wait_recv()
    for f in range(4):
        at, to = f * TH, f * SIDE + 8
        left_f[to:to + TH, :] = jnp.where(col > 0, halo_l[at:at + TH, :].astype(jnp.float32), 0.0)
        right_f[to:to + TH, :] = jnp.where(col < GX - 1, halo_r[at:at + TH, :].astype(jnp.float32), 0.0)

    for ref, r in ((corner_up, 0), (corner_dn, TH - 1)):
        pieces = []
        for f in range(4):
            at = f * SIDE + 8 + r
            pieces += [left_f[at:at + 1, :], right_f[at:at + 1, :]]
        ref[...] = jnp.concatenate(pieces + [jnp.zeros((8, CB), jnp.float32)], axis=0).astype(jnp.bfloat16)
    corner_to_up = remote(corner_up, corner_b, halo_ss.at[4], halo_rs.at[4], up)
    corner_to_down = remote(corner_dn, corner_a, halo_ss.at[5], halo_rs.at[5], down)
    corners = (corner_to_up, corner_to_down)
    for corner in corners:
        corner.start()

    @pl.loop(1, NP)
    def _(q):
        for f in range(4):
            build_sides(xo, f, q, 2 * q)
            build_sides(xe, f, q, 2 * q - 1)

    def rim(side):
        @pl.loop(0, 2)
        def _(i):
            product([(1 + i * HALF, HALF)], RIM, side, RIM_AT + i * HALF_ROWS)
            core(side, half(i)).start()

    def both_ends(side):
        product([(0, 1), (NP - 1, 1)], WHOLE, side, END_AT)
        core(side, end(0)).start()
        core(side, end(1)).start()

    rim(0)
    to_up.wait_recv()
    to_down.wait_recv()
    for corner in corners:
        corner.wait_recv()
    above = jnp.where(row > 0, corner_a[...].astype(jnp.float32), 0.0)
    below = jnp.where(row < GY - 1, corner_b[...].astype(jnp.float32), 0.0)
    for f in range(4):
        xf[pl.ds(place_of(f, -1), TW), :] = jnp.where(row > 0, halo_a[f].astype(jnp.float32)[8:], 0.0)
        xf[pl.ds(place_of(f, TH), TW), :] = jnp.where(row < GY - 1, halo_b[f].astype(jnp.float32)[:TW], 0.0)
        at = f * SIDE + 8
        left_f[at - 1:at, :] = above[2 * f:2 * f + 1]
        right_f[at - 1:at, :] = above[2 * f + 1:2 * f + 2]
        left_f[at + TH:at + TH + 1, :] = below[2 * f:2 * f + 1]
        right_f[at + TH:at + TH + 1, :] = below[2 * f + 1:2 * f + 2]
    for f in range(4):
        for ref, q, r in ((xo, 0, 0), (xe, 0, -1), (xe, NP, TH - 1)):
            build(ref, f, q, r)
            build_sides(ref, f, q, r)

    both_ends(0)
    pass_on(half(0))
    pass_on(half(1))
    rim(1)
    pass_on(end(0))
    pass_on(end(1))
    both_ends(1)
    loads[6].wait()

    def finished(at, n):
        rows = pl.ds(at, n)
        v = keep[1, rows, :] + core_in[1, rows, :] + decode(cross_in[rows, :]) + bias[...]
        return v / (1.0 + jnp.exp(-v))

    def spread(v, f, q, k):
        out_f[pl.ds(f * PIX + q * PAIR + k, SLOT, stride=SLOTS), :] = v

    def settle(f, q):
        at = pl.multiple_of(q * PAIR, 16)
        out[f, pl.ds(at, PAIR), :] = out_f[pl.ds(pl.multiple_of(f * PIX + at, 16), PAIR), :].astype(jnp.bfloat16)

    @pl.loop(0, BLOCKS)
    def _(b):
        core(1, block(b)).wait_recv()
        cross(block(b)).wait_recv()
        v = finished(pl.multiple_of(b * BLOCK_ROWS, 16), BLOCK_ROWS)
        for f in range(2):
            for p in range(BLOCK):
                for k in range(5):
                    at = ((f * BLOCK + p) * 5 + k) * SLOT
                    spread(v[at:at + SLOT], f, 1 + b * BLOCK + p, 1 + k)

    @pl.loop(0, 2)
    def _(i):
        core(1, half(i)).wait_recv()
        cross(half(i)).wait_recv()
        v = finished(pl.multiple_of(RIM_AT + i * HALF_ROWS, 16), HALF_ROWS)
        for s, k in enumerate((0, 6)):
            for f in range(2):
                for p in range(HALF):
                    at = ((s * 2 + f) * HALF + p) * SLOT
                    spread(v[at:at + SLOT], f, 1 + i * HALF + p, k)

    @pl.loop(1, NP - 1)
    def _(q):
        for f in range(2):
            settle(f, q)

    for copy in halos + corners:
        copy.wait_send()

    @pl.loop(0, 2)
    def _(i):
        core(1, end(i)).wait_recv()
        cross(end(i)).wait_recv()
        v = finished(pl.multiple_of(END_AT + i * END_ROWS, 16), END_ROWS)
        q = i * (NP - 1)
        for f in range(2):
            for k in range(SLOTS):
                at = (f * SLOTS + k) * SLOT
                spread(v[at:at + SLOT], f, q, k)
            settle(f, q)

    def sent(part):
        core(0, part).wait_send()
        core(1, part).wait_send()
        cross(part).wait_send()

    @pl.loop(0, BLOCKS)
    def _(b):
        sent(block(b))

    for i in range(2):
        sent(half(i))
        sent(end(i))


def shards(frames, cached, weight, out_bias):
    bf16, f32 = jnp.bfloat16, jnp.float32
    operands = (
        cached.reshape(2, PIX, CB),
        frames.reshape(2, PIX, CB),
        weight.reshape(27 * CB, 4 * CB),
        out_bias.reshape(1, CB),
    )
    out = pl.pallas_call(
        kernel,
        out_shape=jax.ShapeDtypeStruct((2, PIX, CB), bf16),
        in_specs=[pl.BlockSpec(memory_space=pl.ANY)] * 4,
        out_specs=pl.BlockSpec(memory_space=pltpu.VMEM),
        scratch_shapes=[
            pltpu.VMEM((4, PIX, CB), bf16),
            pltpu.VMEM((4 * FRAME, CB), f32),
            pltpu.VMEM((4, NP + 1, WIDE, CB), bf16),
            pltpu.VMEM((4, NP, WIDE, CB), bf16),
            pltpu.VMEM((2, 27 * CB, 2 * CB), bf16),
            pltpu.VMEM((1, CB), f32),
            *[pltpu.VMEM((4 * TH, CB), bf16)] * 4,
            *[pltpu.VMEM((4 * SIDE, CB), f32)] * 2,
            *[pltpu.VMEM((4, 64, CB), bf16)] * 2,
            *[pltpu.VMEM((16, CB), bf16)] * 4,
            *[pltpu.VMEM((2, ROWS, CB), f32)] * 3,
            *[pltpu.VMEM((ROWS, CB), bf16)] * 2,
            pltpu.VMEM((2 * PIX, CB), f32),
            pltpu.SemaphoreType.DMA((7,)),
            *[pltpu.SemaphoreType.DMA((6,))] * 2,
            *[pltpu.SemaphoreType.DMA((2, PARTS))] * 2,
            *[pltpu.SemaphoreType.DMA((PARTS,))] * 2,
        ],
        compiler_params=pltpu.CompilerParams(collective_id=0, has_side_effects=True, vmem_limit_bytes=48 << 20),
        cost_estimate=pl.CostEstimate(flops=2 * 2 * PIX * 27 * CB * 4 * CB, bytes_accessed=7 << 20, transcendentals=2 * PIX * CB),
        name="conv",
    )(*[pltpu.with_memory_space_constraint(x, pltpu.HBM) for x in operands])
    return out.reshape(2, 1, TH, TW, CB)


def solution(mesh):
    in_specs = (
        P(None, "tile", None, None, "ch"),
        P(None, "tile", None, None, "ch"),
        P(None, None, None, "ch", None),
        P("ch"),
    )
    out_specs = P(None, "tile", None, None, "ch")
    return jax.shard_map(shards, mesh=mesh, in_specs=in_specs, out_specs=out_specs, check_vma=False)
```

time: 161 us -> 39 us (0.24)
  waiting for transfers between devices: 92 us -> 0 us
  Pallas kernels: 0 us -> 38 us
  matrix products: 17.3 us -> 0 us
  starting transfers between devices: 16.1 us -> 0 us
  between operations: 13.5 us -> 0.01 us
  local copies, waits for them, and re-layouts: 13.3 us -> 0.93 us
  other arithmetic: 8.62 us -> 0 us
    reduce_scatter x1 -> x0, waiting for transfers between devices: 80.4 us -> none  [shards(): summed = lax.psum_scatter(product[0], 'ch', scatter_dimension=3, tiled=True)]
    pallas_call x0 -> x1, Pallas kernels: none -> 38 us  [shards(): pl.pallas_call(kernel, out_shape=jax.ShapeDtypeStruct((2, PIX, CB), bf16)...]
    conv_general_dilated x1 -> x0, matrix products: 17.3 us -> none  [shards(): lax.conv_general_dilated(window, weight, (1, 1, 1), 'VALID', dimension_nu...]
    ppermute x4 -> x0, starting transfers between devices: 16 us -> none  [passed_along(): return lax.ppermute(x, axis, pairs)]
    ppermute x4 -> x0, waiting for transfers between devices: 11.5 us -> none  [passed_along(): return lax.ppermute(x, axis, pairs)]
    conv_general_dilated x4 -> x0, local copies, waits for them, and re-layouts: 9.44 us -> none  [shards(): lax.conv_general_dilated(window, weight, (1, 1, 1), 'VALID', dimension_nu...]
    broadcast_in_dim x2 -> x0, other arithmetic: 4.76 us -> none  [the longest x1 2.91 us: shards(): return activated[:, None]]
    squeeze x1 -> x0, local copies, waits for them, and re-layouts: 3.84 us -> none  [shards(): summed = lax.psum_scatter(product[0], 'ch', scatter_dimension=3, tiled=True)]
  transfers between devices with their start and end apart: 5 -> 0, of which waited for: 4 -> 0; matrix products, arithmetic and copies ran while one was open for 0% -> 0% of each run, Pallas kernels for 0% -> 0%
where the time goes in v3:
time: 39 us; the launch traced here: 38.9 us
  Pallas kernels  38 us (97%)
  local copies, waits for them, and re-layouts  0.93 us (2%)
    pallas_call x1, Pallas kernels, shards(): pl.pallas_call(kernel, out_shape=jax.ShapeDtypeStruct((2, PIX, CB), bf16)...  38 us
    unnamed x1, local copies, waits for them, and re-layouts  0.93 us

profile of v3, /device:TPU:1, one launch (start us, length us, event | category | flops | bytes accessed | tf_op | source)
XLA Modules:
  0.0 38.9 jit_solution(4762200820858676332)
XLA Ops:
  0.0 38.0 %conv.1 = bf16[2,1792,128]{2,1,0:T(8,128)(2,1)S(1)} custom-call(bf16[2,1792,128]{2,1,0:T(8,128)(2,1)} %bitcast.9, bf16[2,1792,128]{2,1,0:T(8,128)(2,1)} %bitcast.10, bf16[3456,512]{1,0:T(8,128)(2,1)} %bitcast.8, f32[1,128]{1,0:T(1,128)} %bitcast.11), custom_call_target="tpu_custom_call" | custom-call | flops 12683575296 | bytes 7340032 | tf_op jit(solution)/shard_map/conv/pallas_call | solution.py:345
  38.0 0.9 %copy.7 = bf16[2,1,32,56,128]{4,3,2,1,0:T(8,128)(2,1)} copy(bf16[2,1,32,56,128]{4,3,2,1,0:T(8,128)(2,1)S(1)} %bitcast.7) | data formatting | bytes 1835008

commit v4 on v3

--- a/solution.py
+++ b/solution.py
@@ -30,6 +30,7 @@
 END_AT = RIM_AT + MIDDLE * RIM_ROWS
 ROWS = END_AT + 2 * END_ROWS
 BLOCKS = 7
+HALO_AT = 5
 BLOCK = MIDDLE // BLOCKS
 BLOCK_ROWS = BLOCK * INNER_ROWS
 HALF = MIDDLE // 2
@@ -50,7 +51,7 @@
 
 def kernel(cached, frames, weight, bias_in, out, xin, xf, xe, xo, w, bias, edge_l, edge_r, halo_l, halo_r, left_f, right_f,
            halo_a, halo_b, corner_up, corner_dn, corner_a, corner_b, core_out, core_in, keep, cross_out, cross_in, out_f,
-           in_sem, halo_ss, halo_rs, core_ss, core_rs, cross_ss, cross_rs):
+           in_sem, halo_ss, halo_rs, core_ss, core_rs, cross_ss, cross_rs, ready):
     ch = lax.axis_index("ch")
     tile = lax.axis_index("tile")
     h, c = ch // 2, ch % 2
@@ -74,8 +75,15 @@
         load.start()
 
     barrier = pltpu.get_barrier_semaphore()
-    for device in (left, right, up, down, mate, across):
-        pl.semaphore_signal(barrier, inc=1, device_id=device, device_id_type=MESH)
+    first_told = h == c
+
+    def tell(semaphore, device):
+        pl.semaphore_signal(semaphore, inc=1, device_id=device, device_id_type=MESH)
+
+    @pl.when(jnp.logical_not(first_told))
+    def _():
+        tell(barrier, mate)
+        tell(barrier, across)
 
     def remote(src, dst, ss, rs, device):
         return pltpu.make_async_remote_copy(src_ref=src, dst_ref=dst, send_sem=ss, recv_sem=rs, device_id=device, device_id_type=MESH)
@@ -162,7 +170,14 @@
         edge_l[at:at + TH, :] = xf[pl.ds(place_of(f, 0), TH, stride=TW), :].astype(jnp.bfloat16)
         edge_r[at:at + TH, :] = xf[pl.ds(place_of(f, 0) + TW - 1, TH, stride=TW), :].astype(jnp.bfloat16)
 
+    @pl.when(first_told)
+    def _():
+        pl.semaphore_wait(barrier, 2)
+        tell(ready.at[0], mate)
+        tell(ready.at[1], across)
+
     build_all(1, 4)
+
     loads[2].wait()
     loads[3].wait()
     to_left = remote(edge_l, halo_r, halo_ss.at[0], halo_rs.at[0], left)
@@ -182,16 +197,28 @@
 
         product([(1 + b * BLOCK, BLOCK)], INNER, side, b * BLOCK_ROWS)
 
-        @pl.when(j == 0)
-        def _():
-            pl.semaphore_wait(barrier, 6)
-            core(side, block(b)).start()
+        @pl.when((j == 0) & jnp.logical_not(first_told))
+        def _():
+            pl.semaphore_wait(ready.at[0], 1)
+            for device in (left, right, up, down):
+                tell(barrier, device)
+            pl.semaphore_wait(ready.at[1], 1)
+
+        core(side, block(b)).start()
+
+        @pl.when((j == HALO_AT) & jnp.logical_not(first_told))
+        def _():
+            pl.semaphore_wait(barrier, 4)
+            tell(ready.at[2], mate)
+
+        @pl.when((j == HALO_AT) & first_told)
+        def _():
+            pl.semaphore_wait(ready.at[2], 1)
+
+        @pl.when(j == HALO_AT)
+        def _():
             for halo in halos:
                 halo.start()
-
-        @pl.when(j > 0)
-        def _():
-            core(side, block(b)).start()
 
         @pl.when(j < BLOCKS - 1)
         def _():
@@ -365,6 +392,7 @@
             *[pltpu.SemaphoreType.DMA((6,))] * 2,
             *[pltpu.SemaphoreType.DMA((2, PARTS))] * 2,
             *[pltpu.SemaphoreType.DMA((PARTS,))] * 2,
+            pltpu.SemaphoreType.REGULAR((3,)),
         ],
         compiler_params=pltpu.CompilerParams(collective_id=0, has_side_effects=True, vmem_limit_bytes=48 << 20),
         cost_estimate=pl.CostEstimate(flops=2 * 2 * PIX * 27 * CB * 4 * CB, bytes_accessed=7 << 20, transcendentals=2 * PIX * CB),

time: 39 us -> 40 us (1.026)
  Pallas kernels: 38 us -> 39 us
    pallas_call x1, Pallas kernels: 38 us -> 39 us  [shards(): pl.pallas_call(kernel, out_shape=jax.ShapeDtypeStruct((2, PIX, CB), bf16)...]
where the time goes in v4:
time: 40 us; the launch traced here: 39.9 us
  Pallas kernels  39 us (98%)
  local copies, waits for them, and re-layouts  0.93 us (2%)
    pallas_call x1, Pallas kernels, shards(): pl.pallas_call(kernel, out_shape=jax.ShapeDtypeStruct((2, PIX, CB), bf16)...  39 us
    unnamed x1, local copies, waits for them, and re-layouts  0.93 us

profile of v4, /device:TPU:1, one launch (start us, length us, event | category | flops | bytes accessed | tf_op | source)
XLA Modules:
  0.0 39.9 jit_solution(15233589215779987694)
XLA Ops:
  0.0 39.0 %conv.1 = bf16[2,1792,128]{2,1,0:T(8,128)(2,1)S(1)} custom-call(bf16[2,1792,128]{2,1,0:T(8,128)(2,1)} %bitcast.9, bf16[2,1792,128]{2,1,0:T(8,128)(2,1)} %bitcast.10, bf16[3456,512]{1,0:T(8,128)(2,1)} %bitcast.8, f32[1,128]{1,0:T(1,128)} %bitcast.11), custom_call_target="tpu_custom_call" | custom-call | flops 12683575296 | bytes 7340032 | tf_op jit(solution)/shard_map/conv/pallas_call | solution.py:372
  39.0 0.9 %copy.7 = bf16[2,1,32,56,128]{4,3,2,1,0:T(8,128)(2,1)} copy(bf16[2,1,32,56,128]{4,3,2,1,0:T(8,128)(2,1)S(1)} %bitcast.7) | data formatting | bytes 1835008

commit v5 on v4

--- a/solution.py
+++ b/solution.py
@@ -30,7 +30,9 @@
 END_AT = RIM_AT + MIDDLE * RIM_ROWS
 ROWS = END_AT + 2 * END_ROWS
 BLOCKS = 7
+SIDE_AT = 1
 HALO_AT = 5
+CORNER_AT = 6
 BLOCK = MIDDLE // BLOCKS
 BLOCK_ROWS = BLOCK * INNER_ROWS
 HALF = MIDDLE // 2
@@ -186,6 +188,10 @@
     to_down = remote(xin.at[:, pl.ds(PIX - 64, 64)], halo_a, halo_ss.at[3], halo_rs.at[3], down)
     halos = (to_left, to_right, to_up, to_down)
 
+    corner_to_up = remote(corner_up, corner_b, halo_ss.at[4], halo_rs.at[4], up)
+    corner_to_down = remote(corner_dn, corner_a, halo_ss.at[5], halo_rs.at[5], down)
+    corners = (corner_to_up, corner_to_down)
+
     @pl.loop(0, 2 * BLOCKS)
     def _(j):
         side, b = j // BLOCKS, j % BLOCKS
@@ -200,25 +206,35 @@
         @pl.when((j == 0) & jnp.logical_not(first_told))
         def _():
             pl.semaphore_wait(ready.at[0], 1)
-            for device in (left, right, up, down):
-                tell(barrier, device)
             pl.semaphore_wait(ready.at[1], 1)
 
+            @pl.when(ch == 1)
+            def _():
+                tell(barrier, left)
+                tell(barrier, right)
+
+            @pl.when(ch == 2)
+            def _():
+                tell(barrier, up)
+                tell(barrier, down)
+
         core(side, block(b)).start()
 
-        @pl.when((j == HALO_AT) & jnp.logical_not(first_told))
-        def _():
-            pl.semaphore_wait(barrier, 4)
-            tell(ready.at[2], mate)
-
-        @pl.when((j == HALO_AT) & first_told)
-        def _():
-            pl.semaphore_wait(ready.at[2], 1)
-
-        @pl.when(j == HALO_AT)
-        def _():
-            for halo in halos:
-                halo.start()
+        for step, asks, at, pair in ((SIDE_AT, 1, 2, halos[:2]), (HALO_AT, 2, 3, halos[2:])):
+            @pl.when((j == step) & (ch == asks))
+            def _():
+                pl.semaphore_wait(barrier, 2)
+                for device in (mate, across, (3 - asks, tile)):
+                    tell(ready.at[at], device)
+
+            @pl.when((j == step) & (ch != asks))
+            def _():
+                pl.semaphore_wait(ready.at[at], 1)
+
+            @pl.when(j == step)
+            def _():
+                for halo in pair:
+                    halo.start()
 
         @pl.when(j < BLOCKS - 1)
         def _():
@@ -228,24 +244,23 @@
         def _():
             pass_on(block(j - 1))
 
-    to_left.wait_recv()
-    to_right.wait_recv()
-    for f in range(4):
-        at, to = f * TH, f * SIDE + 8
-        left_f[to:to + TH, :] = jnp.where(col > 0, halo_l[at:at + TH, :].astype(jnp.float32), 0.0)
-        right_f[to:to + TH, :] = jnp.where(col < GX - 1, halo_r[at:at + TH, :].astype(jnp.float32), 0.0)
-
-    for ref, r in ((corner_up, 0), (corner_dn, TH - 1)):
-        pieces = []
-        for f in range(4):
-            at = f * SIDE + 8 + r
-            pieces += [left_f[at:at + 1, :], right_f[at:at + 1, :]]
-        ref[...] = jnp.concatenate(pieces + [jnp.zeros((8, CB), jnp.float32)], axis=0).astype(jnp.bfloat16)
-    corner_to_up = remote(corner_up, corner_b, halo_ss.at[4], halo_rs.at[4], up)
-    corner_to_down = remote(corner_dn, corner_a, halo_ss.at[5], halo_rs.at[5], down)
-    corners = (corner_to_up, corner_to_down)
-    for corner in corners:
-        corner.start()
+        @pl.when(j == CORNER_AT)
+        def _():
+            to_left.wait_recv()
+            to_right.wait_recv()
+            for f in range(4):
+                at, to = f * TH, f * SIDE + 8
+                left_f[to:to + TH, :] = jnp.where(col > 0, halo_l[at:at + TH, :].astype(jnp.float32), 0.0)
+                right_f[to:to + TH, :] = jnp.where(col < GX - 1, halo_r[at:at + TH, :].astype(jnp.float32), 0.0)
+
+            for ref, r in ((corner_up, 0), (corner_dn, TH - 1)):
+                pieces = []
+                for f in range(4):
+                    at = f * SIDE + 8 + r
+                    pieces += [left_f[at:at + 1, :], right_f[at:at + 1, :]]
+                ref[...] = jnp.concatenate(pieces + [jnp.zeros((8, CB), jnp.float32)], axis=0).astype(jnp.bfloat16)
+            for corner in corners:
+                corner.start()
 
     @pl.loop(1, NP)
     def _(q):
@@ -392,7 +407,7 @@
             *[pltpu.SemaphoreType.DMA((6,))] * 2,
             *[pltpu.SemaphoreType.DMA((2, PARTS))] * 2,
             *[pltpu.SemaphoreType.DMA((PARTS,))] * 2,
-            pltpu.SemaphoreType.REGULAR((3,)),
+            pltpu.SemaphoreType.REGULAR((4,)),
         ],
         compiler_params=pltpu.CompilerParams(collective_id=0, has_side_effects=True, vmem_limit_bytes=48 << 20),
         cost_estimate=pl.CostEstimate(flops=2 * 2 * PIX * 27 * CB * 4 * CB, bytes_accessed=7 << 20, transcendentals=2 * PIX * CB),

time: 40 us -> 41 us (1.025)
  the two profiles are of different devices: /device:TPU:1 before, /device:TPU:6 now
where the time goes in v5:
time: 41 us; the launch traced here: 40.9 us
  Pallas kernels  40 us (98%)
  local copies, waits for them, and re-layouts  0.93 us (2%)
    pallas_call x1, Pallas kernels, shards(): pl.pallas_call(kernel, out_shape=jax.ShapeDtypeStruct((2, PIX, CB), bf16)...  40 us
    unnamed x1, local copies, waits for them, and re-layouts  0.93 us

profile of v5, /device:TPU:6, one launch (start us, length us, event | category | flops | bytes accessed | tf_op | source)
XLA Modules:
  0.0 40.9 jit_solution(14427848666952700227)
XLA Ops:
  0.0 40.0 %conv.1 = bf16[2,1792,128]{2,1,0:T(8,128)(2,1)S(1)} custom-call(bf16[2,1792,128]{2,1,0:T(8,128)(2,1)} %bitcast.9, bf16[2,1792,128]{2,1,0:T(8,128)(2,1)} %bitcast.10, bf16[3456,512]{1,0:T(8,128)(2,1)} %bitcast.8, f32[1,128]{1,0:T(1,128)} %bitcast.11), custom_call_target="tpu_custom_call" | custom-call | flops 12683575296 | bytes 7340032 | tf_op jit(solution)/shard_map/conv/pallas_call | solution.py:387
  40.0 0.9 %copy.7 = bf16[2,1,32,56,128]{4,3,2,1,0:T(8,128)(2,1)} copy(bf16[2,1,32,56,128]{4,3,2,1,0:T(8,128)(2,1)S(1)} %bitcast.7) | data formatting | bytes 1835008

commit v6 on v3

--- a/solution.py
+++ b/solution.py
@@ -30,6 +30,7 @@
 END_AT = RIM_AT + MIDDLE * RIM_ROWS
 ROWS = END_AT + 2 * END_ROWS
 BLOCKS = 7
+CORNER_AT = 5
 BLOCK = MIDDLE // BLOCKS
 BLOCK_ROWS = BLOCK * INNER_ROWS
 HALF = MIDDLE // 2
@@ -171,6 +172,10 @@
     to_down = remote(xin.at[:, pl.ds(PIX - 64, 64)], halo_a, halo_ss.at[3], halo_rs.at[3], down)
     halos = (to_left, to_right, to_up, to_down)
 
+    corner_to_up = remote(corner_up, corner_b, halo_ss.at[4], halo_rs.at[4], up)
+    corner_to_down = remote(corner_dn, corner_a, halo_ss.at[5], halo_rs.at[5], down)
+    corners = (corner_to_up, corner_to_down)
+
     @pl.loop(0, 2 * BLOCKS)
     def _(j):
         side, b = j // BLOCKS, j % BLOCKS
@@ -201,24 +206,23 @@
         def _():
             pass_on(block(j - 1))
 
-    to_left.wait_recv()
-    to_right.wait_recv()
-    for f in range(4):
-        at, to = f * TH, f * SIDE + 8
-        left_f[to:to + TH, :] = jnp.where(col > 0, halo_l[at:at + TH, :].astype(jnp.float32), 0.0)
-        right_f[to:to + TH, :] = jnp.where(col < GX - 1, halo_r[at:at + TH, :].astype(jnp.float32), 0.0)
-
-    for ref, r in ((corner_up, 0), (corner_dn, TH - 1)):
-        pieces = []
-        for f in range(4):
-            at = f * SIDE + 8 + r
-            pieces += [left_f[at:at + 1, :], right_f[at:at + 1, :]]
-        ref[...] = jnp.concatenate(pieces + [jnp.zeros((8, CB), jnp.float32)], axis=0).astype(jnp.bfloat16)
-    corner_to_up = remote(corner_up, corner_b, halo_ss.at[4], halo_rs.at[4], up)
-    corner_to_down = remote(corner_dn, corner_a, halo_ss.at[5], halo_rs.at[5], down)
-    corners = (corner_to_up, corner_to_down)
-    for corner in corners:
-        corner.start()
+        @pl.when(j == CORNER_AT)
+        def _():
+            to_left.wait_recv()
+            to_right.wait_recv()
+            for f in range(4):
+                at, to = f * TH, f * SIDE + 8
+                left_f[to:to + TH, :] = jnp.where(col > 0, halo_l[at:at + TH, :].astype(jnp.float32), 0.0)
+                right_f[to:to + TH, :] = jnp.where(col < GX - 1, halo_r[at:at + TH, :].astype(jnp.float32), 0.0)
+
+            for ref, r in ((corner_up, 0), (corner_dn, TH - 1)):
+                pieces = []
+                for f in range(4):
+                    at = f * SIDE + 8 + r
+                    pieces += [left_f[at:at + 1, :], right_f[at:at + 1, :]]
+                ref[...] = jnp.concatenate(pieces + [jnp.zeros((8, CB), jnp.float32)], axis=0).astype(jnp.bfloat16)
+            for corner in corners:
+                corner.start()
 
     @pl.loop(1, NP)
     def _(q):

time: 39 us -> 38.7 us (level)
  no operation moved by 1% of the time
where the time goes in v6:
time: 38.7 us
  Pallas kernels  37.7 us (97%)
  local copies, waits for them, and re-layouts  0.93 us (2%)
    pallas_call x1, Pallas kernels, shards(): pl.pallas_call(kernel, out_shape=jax.ShapeDtypeStruct((2, PIX, CB), bf16)...  37.7 us
    unnamed x1, local copies, waits for them, and re-layouts  0.93 us

profile of v6, /device:TPU:1, one launch (start us, length us, event | category | flops | bytes accessed | tf_op | source)
XLA Modules:
  0.0 38.7 jit_solution(3404288625347399987)
XLA Ops:
  0.0 37.7 %conv.1 = bf16[2,1792,128]{2,1,0:T(8,128)(2,1)S(1)} custom-call(bf16[2,1792,128]{2,1,0:T(8,128)(2,1)} %bitcast.9, bf16[2,1792,128]{2,1,0:T(8,128)(2,1)} %bitcast.10, bf16[3456,512]{1,0:T(8,128)(2,1)} %bitcast.8, f32[1,128]{1,0:T(1,128)} %bitcast.11), custom_call_target="tpu_custom_call" | custom-call | flops 12683575296 | bytes 7340032 | tf_op jit(solution)/shard_map/conv/pallas_call | solution.py:349
  37.7 0.9 %copy.7 = bf16[2,1,32,56,128]{4,3,2,1,0:T(8,128)(2,1)} copy(bf16[2,1,32,56,128]{4,3,2,1,0:T(8,128)(2,1)S(1)} %bitcast.7) | data formatting | bytes 1835008
